TPU v7x, 32 devices: a whole 2x2x4 slice. The times are simulated.
32 devices in a mesh: groups: 2 (over x), ctx: 16 (over z, y, core).
Axes of the slice: x: 2, y: 2, z: 4, core: 2. Of those that a mesh axis runs over, the one named last changes fastest.
Arguments:
- context: bfloat16 [96, 256, 1024], P(('groups', 'ctx')), parts along dimension 0, may hold values from -6 to 6
- counts: int32 [32], P('groups'), parts along dimension 0, may hold values from 1 to 3, as said below
- queries: bfloat16 [128, 4096], P(('groups', 'ctx')), parts along dimension 0, may hold values from -120 to 120
- norm_gain: bfloat16 [1024], replicated, may hold values from 0.099609375 to 1.8984375
- w_query: bfloat16 [1024, 1024], replicated, may hold values from -1 to 1
- w_key: bfloat16 [1024, 1024], replicated, may hold values from -9 to 9
- w_value: bfloat16 [1024, 1024], replicated, may hold values from -0.1875 to 0.1875
- w_out: bfloat16 [1024, 1024], replicated, may hold values from -0.1875 to 0.1875
- final_gain: bfloat16 [1024], replicated, may hold values from 0.099609375 to 1.8984375
- w_kv: bfloat16 [1024, 2048], P(None, 'ctx'), may hold values from -0.1875 to 0.1875
Outputs:
- attended_context: bfloat16 [128, 4096], P(('groups', 'ctx')), parts along dimension 0
There are 2 independent parts, one for each index of `groups`. A program takes and returns all parts, laid end to end along the dimension named above; an argument that names none is the same for every part. Nothing has to cross between parts.
Inputs may be any that keep to these rules, and one draw needn't show every extreme that they name: Device d's slots are d * 3 to d * 3 + 2, and only the first counts[d] of them hold live blocks. The largest count equals 3 in every draw. For every d below 8, counts[d] + counts[d + 8] is at most 4, and equals it for some d in every draw.
All inputs are finite; a program needn't handle non-finite values.
Results may differ from a plain program's by a relative error of at most 0.025.
The roundings to bfloat16 on the way count: a program that leaves them out, or rounds other values in their place, can miss the bound.
Values may be sent and summed in bfloat16 or wider, within the bound.
No kernel may reach another device: no remote copies, remote signals or barrier semaphores. Data moves between devices by JAX's collectives and lax.ppermute only.
A program may use at most 128 MiB of HBM per device.

v0:
```python
import math

import jax
import jax.numpy as jnp
from jax import lax
from jax.sharding import PartitionSpec as P

D_ENC = 1024
ENC_HEADS = 16
ENC_HD = 64
BLOCK = 256
KV_HEADS = 8
HEAD_DIM = 128
Q_HEADS = 32
GROUP = 4
QW = 4096
CAP = 3


def root_scale(values, gain):
    values = values.astype(jnp.float32)
    return (
        values
        * lax.rsqrt(jnp.mean(values * values, axis=-1, keepdims=True) + 1e-05)
        * gain.astype(jnp.float32)
    )


def rotary_tables(length, head_width):
    position = jnp.arange(length).astype(jnp.float32)[:, None]
    frequency = jnp.exp(
        jnp.arange(head_width // 2).astype(jnp.float32) * (-2.0 * math.log(10000.0) / head_width)
    )
    phase_angle = position * frequency[None, :]
    return (jnp.cos(phase_angle)[:, None, :], jnp.sin(phase_angle)[:, None, :])


def rotate(values, cosine_table, sine_table):
    half_width = values.shape[-1] // 2
    lower_half = values[..., :half_width]
    upper_half = values[..., half_width:]
    return jnp.concatenate(
        [
            lower_half * cosine_table - upper_half * sine_table,
            upper_half * cosine_table + lower_half * sine_table,
        ],
        axis=-1,
    )


def weighted_sums(cross_scores, top_scores, key_alive, cross_values):
    cross_weights = jnp.where(key_alive, jnp.exp(cross_scores - top_scores[..., None]), 0.0)
    total_rows = cross_scores.shape[0]
    denominator = jnp.sum(cross_weights, axis=-1).reshape(total_rows, Q_HEADS)
    numerator = jnp.einsum(
        "rkgt,tkd->rkgd",
        cross_weights.astype(jnp.bfloat16),
        cross_values,
        preferred_element_type=jnp.float32,
    )
    return (numerator.reshape(total_rows, QW), denominator)


def local(context, counts, queries, norm_gain, w_query, w_key, w_value, w_out, final_gain, w_kv):
    places = lax.axis_size("ctx")
    device_index = lax.axis_index("ctx")
    device_number = jnp.arange(places)
    own_count = jnp.sum(jnp.where(device_number == device_index, counts, 0))
    alive_slot = jnp.arange(CAP) < own_count
    slot_count = context.shape[0]
    row_count = slot_count * BLOCK
    normed = root_scale(context, norm_gain).astype(jnp.bfloat16).reshape(row_count, D_ENC)
    cosine_table, sine_table = rotary_tables(BLOCK, ENC_HD)

    def project(weight):
        return jnp.dot(normed, weight, preferred_element_type=jnp.float32).reshape(
            slot_count, BLOCK, ENC_HEADS, ENC_HD
        )

    query_rows = rotate(project(w_query), cosine_table, sine_table).astype(jnp.bfloat16)
    key_rows = rotate(project(w_key), cosine_table, sine_table).astype(jnp.bfloat16)
    value_rows = project(w_value).astype(jnp.bfloat16)
    scores = jnp.einsum(
        "sqhd,skhd->shqk", query_rows, key_rows, preferred_element_type=jnp.float32
    ) / math.sqrt(ENC_HD)
    weights = jax.nn.softmax(scores, axis=-1).astype(jnp.bfloat16)
    mixed_rows = jnp.einsum(
        "shqk,skhd->sqhd", weights, value_rows, preferred_element_type=jnp.float32
    )
    mixed_rows = mixed_rows.astype(jnp.bfloat16).reshape(row_count, D_ENC)
    residual = context.reshape(row_count, D_ENC).astype(jnp.float32) + jnp.dot(
        mixed_rows, w_out, preferred_element_type=jnp.float32
    )
    final_norm = root_scale(residual, final_gain).astype(jnp.bfloat16)
    key_value = jnp.dot(
        final_norm,
        lax.all_gather(w_kv, "ctx", axis=1, tiled=True),
        preferred_element_type=jnp.float32,
    ).astype(jnp.bfloat16)
    cross_keys = key_value[:, : KV_HEADS * HEAD_DIM].reshape(row_count, KV_HEADS, HEAD_DIM)
    cross_values = key_value[:, KV_HEADS * HEAD_DIM :].reshape(row_count, KV_HEADS, HEAD_DIM)
    every_query = lax.all_gather(queries, "ctx", axis=0, tiled=True)
    total_rows = every_query.shape[0]
    grouped = every_query.reshape(total_rows, KV_HEADS, GROUP, HEAD_DIM)
    cross_scores = jnp.einsum(
        "rkgd,tkd->rkgt", grouped, cross_keys, preferred_element_type=jnp.float32
    ) / math.sqrt(HEAD_DIM)
    key_alive = jnp.repeat(alive_slot, BLOCK)
    local_top = jnp.max(jnp.where(key_alive, cross_scores, -jnp.inf), axis=-1)
    row_top = lax.pmax(local_top.astype(jnp.bfloat16), "ctx").astype(local_top.dtype)
    numerator, denominator = weighted_sums(cross_scores, row_top, key_alive, cross_values)
    own_numerator, own_denominator = (
        lax.psum_scatter(numerator, "ctx", scatter_dimension=0, tiled=True),
        lax.psum_scatter(denominator, "ctx", scatter_dimension=0, tiled=True),
    )
    own_rows = own_numerator.shape[0]
    result = own_numerator.reshape(own_rows, Q_HEADS, HEAD_DIM) / own_denominator[..., None]
    return result.reshape(own_rows, QW).astype(jnp.bfloat16)


def solution(mesh):
    in_specs = (
        P(("groups", "ctx"), None, None),
        P("groups"),
        P(("groups", "ctx"), None),
        P(),
        P(),
        P(),
        P(),
        P(),
        P(),
        P(None, "ctx"),
    )
    out_specs = P(("groups", "ctx"), None)
    return jax.shard_map(local, mesh=mesh, in_specs=in_specs, out_specs=out_specs, check_vma=False)
```

profile of v0, /device:TPU:0, one launch (start us, length us, event | category | flops | bytes accessed | tf_op | source)
XLA Modules:
  0.0 249.6 jit_solution(10173682947700070167)
XLA Ops:
  8.0 4.0 %copy.28 = bf16[1024,1024]{0,1:T(8,128)(2,1)} copy(bf16[1024,1024]{1,0:T(8,128)(2,1)} %param.15) | data formatting | bytes 4194304 | tf_op args[5]
  12.0 4.0 %copy.27 = bf16[1024,1024]{0,1:T(8,128)(2,1)} copy(bf16[1024,1024]{1,0:T(8,128)(2,1)} %param.14) | data formatting | bytes 4194304 | tf_op args[4]
  15.9 3.9 %copy.26 = bf16[1024,1024]{0,1:T(8,128)(2,1)} copy(bf16[1024,1024]{1,0:T(8,128)(2,1)} %param.16) | data formatting | bytes 4194304 | tf_op args[6]
  19.9 1.8 multiply_reduce_fusion.2
  21.9 4.1 %fusion.38 = f32[3,256,16,64]{1,3,2,0:T(8,128)S(1)} fusion(bf16[16,64,1024,1]{2,1,0,3:T(8,128)(2,1)} %bitcast.80, bf16[3,256,1024]{2,1,0:T(8,128)(2,1)} %param.10, f32[1024]{0:T(1024)S(1)} %convert_element_type.95, f32[3,256]{1,0:T(4,128)S(1)} %add_rsqrt_fusion.1), kind=kOutput, calls=%fused_computation.49 | convolution fusion | flops 1613758464 | bytes 6822912 | tf_op jit(solution)/shard_map/dot_general | solution.py:76
  26.1 1.9 fusion.40
  29.2 6.3 %fusion.19 = f32[3,16,256,256]{2,3,1,0:T(8,128)} fusion(bf16[3,256,16,32]{1,3,2,0:T(8,128)(2,1)S(1)} %get-tuple-element.11, bf16[3,256,16,32]{1,3,2,0:T(8,128)(2,1)S(1)} %get-tuple-element.12, bf16[3,256,16,32]{1,3,2,0:T(8,128)(2,1)S(1)} %get-tuple-element.6, bf16[3,256,16,32]{1,3,2,0:T(8,128)(2,1)S(1)} %get-tuple-element.5), kind=kOutput, calls=%fused_computation.30 | convolution fusion | flops 408944640 | bytes 15728640 | tf_op jit(solution)/shard_map/sqhd,skhd->shqk/dot_general | solution.py:83
  35.5 16.4 %fusion.50 = (f32[3,16,256]{2,1,0:T(8,128)S(1)}, f32[3,16,256,256]{2,3,1,0:T(8,128)}) fusion(f32[3,16,256,256]{2,3,1,0:T(8,128)} %fusion.19), kind=kOutput, calls=%fused_computation.68 | output fusion | flops 12583167 | bytes 25214976 | tf_op jit(solution)/shard_map/sub | solution.py:86
  51.8 10.0 %fusion.31 = bf16[3,256,16,64]{1,3,2,0:T(8,128)(2,1)} fusion(f32[3,16,256,256]{2,3,1,0:T(8,128)} %get-tuple-element.16, f32[3,16,256]{2,1,0:T(8,128)S(1)} %get-tuple-element.15, bf16[16,64,1024,1]{2,1,0,3:T(8,128)(2,1)} %bitcast.78, bf16[3,256,1024]{2,1,0:T(8,128)(2,1)} %param.10, f32[1024]{0:T(1024)S(1)} %convert_element_type.95, ...), kind=kOutput, calls=%fused_computation.46 | convolution fusion | flops 2024275968 | bytes 17882112 | tf_op jit(solution)/shard_map/shqk,skhd->sqhd/dot_general | solution.py:87
  61.9 3.0 %copy.30 = bf16[3,256,16,64]{1,0,3,2:T(4,128)(2,1)S(1)} copy(bf16[3,256,16,64]{1,3,2,0:T(8,128)(2,1)} %fusion.31) | data formatting | bytes 3145728 | tf_op jit(solution)/shard_map/convert_element_type | solution.py:90
  64.9 1.5 copy.46
  67.8 24.6 %all-gather = bf16[16,4,4096]{2,1,0:T(4,128)(2,1)S(1)} all-gather(bf16[1,4,4096]{2,1,0:T(4,128)(2,1)S(1)} %bitcast.85), channel_id=1, replica_groups=mesh['groups'=2,'ctx'=16] {'ctx'}, dimensions={0}, use_global_device_ids=true | all-gather | bytes 557056 | tf_op jit(solution)/shard_map/all_gather | solution.py:102
  94.1 5.5 %multiply_reduce_fusion.1 = (f32[768]{0:T(1024)S(1)}, f32[768,1024]{1,0:T(8,128)}) fusion(bf16[768,1024]{0,1:T(8,128)(2,1)} %bitcast.81, bf16[1024,1024]{1,0:T(8,128)(2,1)S(1)} %copy-done, bf16[3,256,1024]{2,1,0:T(8,128)(2,1)} %param.10), kind=kOutput, calls=%fused_computation.21 | convolution fusion | flops 1613757696 | bytes 8391680 | tf_op jit(solution)/shard_map/dot_general | solution.py:91
  99.6 6.6 %convolution_convert_fusion = bf16[768,2048]{1,0:T(8,128)(2,1)S(1)} fusion(bf16[1024,2048]{1,0:T(8,128)(2,1)} %all-gather.3.cloned.1.call-done, f32[768,1024]{1,0:T(8,128)} %get-tuple-element.18, f32[1024]{0:T(1024)S(1)} %convert_element_type.103, f32[768]{0:T(1024)S(1)} %add_rsqrt_fusion), kind=kOutput, calls=%fused_computation.14 | convolution fusion | flops 3225157632 | bytes 10492928 | tf_op jit(solution)/shard_map/dot_general | solution.py:95
  106.3 1.8 slice_bitcast_fusion.1
  108.6 3.9 %fusion.4 = (bf16[64,8,4]{0,2,1:T(4,128)(2,1)S(1)}, f32[8,768,64,4]{1,2,3,0:T(8,128)}) fusion(pred[768]{0:T(1024)(128)(4,1)S(1)} %reshape.127, bf16[64,8,4,128]{3,2,1,0:T(4,128)(2,1)S(1)} %reshape.129, bf16[768,8,128,1]{2,1,0,3:T(8,128)(2,1)S(1)} %bitcast.82), kind=kOutput, calls=%fused_computation.7 | convolution fusion | flops 407369728 | bytes 8393472 | tf_op jit(solution)/shard_map/rkgd,tkd->rkgt/dot_general | solution.py:105
  112.4 30.4 %pmax.7 = bf16[64,8,4]{0,2,1:T(4,128)(2,1)S(1)} all-reduce(bf16[64,8,4]{0,2,1:T(4,128)(2,1)S(1)} %get-tuple-element.19), channel_id=1, replica_groups=mesh['groups'=2,'ctx'=16] {'ctx'}, use_global_device_ids=true, to_apply=%region_6.7 | all-reduce | flops 2048 | bytes 8192 | tf_op jit(solution)/shard_map/pmax | solution.py:110
  142.8 1.9 copy.47
  144.7 3.7 %fusion.32 = f32[64,8,4,128]{3,0,2,1:T(8,128)S(1)} fusion(f32[8,768,64,4]{1,2,3,0:T(8,128)} %get-tuple-element.20, f32[64,8,4]{0,2,1:T(4,128)S(1)} %convert_element_type.107, pred[768]{0:T(1024)(128)(4,1)S(1)} %reshape.127, bf16[768,8,128,1]{2,1,0,3:T(8,128)(2,1)S(1)} %bitcast.83), kind=kOutput, calls=%fused_computation.47 | convolution fusion | flops 408944640 | bytes 8921856 | tf_op jit(solution)/shard_map/rkgt,tkd->rkgd/dot_general | solution.py:55
  149.0 1.4 reshape.130
  150.4 3.7 %fusion.9 = f32[64,8,4]{0,2,1:T(4,128)S(1)} fusion(f32[8,768,64,4]{1,2,3,0:T(8,128)} %get-tuple-element.20, f32[64,8,4]{0,2,1:T(4,128)S(1)} %convert_element_type.107, pred[768]{0:T(1024)(128)(4,1)S(1)} %reshape.127), kind=kLoop, calls=%fused_computation.12 | loop fusion | flops 6289408 | bytes 6308608 | tf_op jit(solution)/shard_map/reduce_sum | solution.py:54
  154.1 58.0 %all-reduce.1 = f32[64,32]{0,1:T(8,128)S(1)} all-reduce(f32[64,32]{0,1:T(8,128)S(1)} %bitcast.84), channel_id=3, replica_groups=mesh['groups'=2,'ctx'=16] {'ctx'}, use_global_device_ids=true, to_apply=%region_9.10.clone | all-reduce | flops 2048 | bytes 16384
  212.4 28.8 %all-reduce.4.cloned.1.call-done = f32[64,4096]{1,0:T(8,128)} async-done(((f32[64,4096]{1,0:T(8,128)}), f32[64,4096]{1,0:T(8,128)}) %all-reduce.4.cloned.1.call-update) | async-done | bytes 1048592
  241.2 1.6 fusion.44
  (39 shorter events, 6.7 us)
Async XLA Ops:
  6.5 87.6 %copy-start = (bf16[1024,1024]{1,0:T(8,128)(2,1)S(1)}, bf16[1024,1024]{1,0:T(8,128)(2,1)}, u32[]{:S(2)}) copy-start(bf16[1024,1024]{1,0:T(8,128)(2,1)} %param.17) | copy-start | bytes 6291460
  6.5 93.1 %all-gather.3.cloned.1.call-start = ((), (), s32[]{:S(2)}) async-start(), calls=%async_computation | async-start | bytes 4456448 | tf_op jit(solution)/shard_map/all_gather | solution.py:97
  7.3 234.0 %all-reduce.4.cloned.1.call-start = ((), (), s32[]{:S(2)}) async-start(), calls=%async_computation.1 | async-start | bytes 2097152
  21.9 4.1 %copy-start.1 = (bf16[1024,1024]{0,1:T(8,128)(2,1)S(1)}, bf16[1024,1024]{0,1:T(8,128)(2,1)}, u32[]{:S(2)}) copy-start(bf16[1024,1024]{0,1:T(8,128)(2,1)} %copy.27) | copy-start | bytes 6291460
  21.9 4.1 %copy-start.2 = (bf16[3,256,1024]{2,1,0:T(8,128)(2,1)S(1)}, bf16[3,256,1024]{2,1,0:T(8,128)(2,1)}, u32[]{:S(2)}) copy-start(bf16[3,256,1024]{2,1,0:T(8,128)(2,1)} %param.10) | copy-start | bytes 4718596
  61.9 4.5 %copy-start.4 = (bf16[1024]{0:T(1024)(128)(2,1)S(1)}, bf16[1024]{0:T(1024)(128)(2,1)}, u32[]{:S(2)}) copy-start(bf16[1024]{0:T(1024)(128)(2,1)} %param.18) | copy-start | bytes 6148
  61.9 4.5 %copy-start.5 = (s32[16]{0:T(128)S(1)}, s32[16]{0:T(128)}, u32[]{:S(2)}) copy-start(s32[16]{0:T(128)} %param.11) | copy-start | bytes 196
  61.9 5.9 %copy-start.3 = (bf16[4,4096]{1,0:T(4,128)(2,1)S(1)}, bf16[4,4096]{1,0:T(4,128)(2,1)}, u32[]{:S(2)}) copy-start(bf16[4,4096]{1,0:T(4,128)(2,1)} %param.12) | copy-start | bytes 98308
  64.8 28.0 %copy-start.6 = (u32[32]{0:T(128)S(1)}, u32[32]{0:T(128)}, u32[]{:S(2)}) copy-start(u32[32]{0:T(128)} %constant.31) | copy-start | bytes 388
Sparse Core Ops, SparseCore 0:
  9.5 55.9 all-gather.2
  150.6 90.6 all-reduce.3
where the time goes:
time: 250 us
  blocking collectives  113 us (45%)
  matrix products  42 us (17%)
  waiting for transfers between devices  29.6 us (12%)
  other arithmetic  26.8 us (11%)
  local copies, waits for them, and re-layouts  24 us (10%)
  between operations  14.2 us (6%)
    unnamed x1, blocking collectives  58 us
    pmax x1, blocking collectives, local(): lax.pmax(local_top.astype(jnp.bfloat16), 'ctx').astype(local_top.dtype)  30.4 us
    unnamed x3, waiting for transfers between devices  29.6 us
    all_gather x1, blocking collectives, local(): every_query = lax.all_gather(queries, 'ctx', axis=0, tiled=True)  24.6 us
    unnamed x24, local copies, waits for them, and re-layouts  18.2 us
    sub x1, other arithmetic, local(): weights = jax.nn.softmax(scores, axis=-1).astype(jnp.bfloat16)  16.4 us
    dot_general x1, matrix products, local(): jnp.einsum('shqk,skhd->sqhd', weights, value_rows, preferred_element_type...  10 us
    dot_general x1, matrix products, local(): jnp.dot(final_norm, lax.all_gather(w_kv, 'ctx', axis=1, tiled=True), pref...  6.61 us
  transfers between devices with their start and end apart: 2, of which 1 were waited for; matrix products, arithmetic and copies ran while one was open for 28% of the time, Pallas kernels for 0%

commit v1 on v0

--- a/solution.py
+++ b/solution.py
@@ -1,8 +1,11 @@
+import functools
 import math
 
 import jax
 import jax.numpy as jnp
 from jax import lax
+from jax.experimental import pallas as pl
+from jax.experimental.pallas import tpu as pltpu
 from jax.sharding import PartitionSpec as P
 
 D_ENC = 1024
@@ -15,15 +18,265 @@
 GROUP = 4
 QW = 4096
 CAP = 3
+HALF_HEADS = KV_HEADS // 2
+LANES = 128
+F32 = jnp.float32
+BF16 = jnp.bfloat16
+VMEM = pl.BlockSpec(memory_space=pltpu.VMEM)
+SMEM = pl.BlockSpec(memory_space=pltpu.SMEM)
 
 
 def root_scale(values, gain):
-    values = values.astype(jnp.float32)
+    values = values.astype(F32)
     return (
         values
         * lax.rsqrt(jnp.mean(values * values, axis=-1, keepdims=True) + 1e-05)
-        * gain.astype(jnp.float32)
-    )
+        * gain.astype(F32)
+    )
+
+
+def rotary_lanes():
+    position = jnp.arange(BLOCK).astype(F32)[:, None]
+    frequency = jnp.exp(jnp.arange(ENC_HD // 2).astype(F32) * (-2.0 * math.log(10000.0) / ENC_HD))
+    angle = position * frequency[None, :]
+    cosine, sine = jnp.cos(angle), jnp.sin(angle)
+    return (
+        jnp.concatenate([cosine, cosine, cosine, cosine], axis=1),
+        jnp.concatenate([-sine, sine, -sine, sine], axis=1),
+    )
+
+
+def encoder_kernel(alive_ref, x_ref, alt_ref, wq_ref, wk_ref, wv_ref, wo_ref, gain_ref, fgain_ref,
+                   cos_ref, sin_ref, out_ref, mixed_ref):
+    @pl.when(alive_ref[0] != 0)
+    def _():
+        block = jnp.where(alive_ref[1] != 0, alt_ref[...], x_ref[...])
+        normed = root_scale(block, gain_ref[...]).astype(BF16)
+        cosine, sine = cos_ref[...], sin_ref[...]
+        lane = lax.broadcasted_iota(jnp.int32, (BLOCK, LANES), 1)
+        lower = (lane % ENC_HD) < ENC_HD // 2
+        first = lane < ENC_HD
+
+        def rotate(values):
+            swapped = jnp.where(
+                lower,
+                pltpu.roll(values, LANES - ENC_HD // 2, 1),
+                pltpu.roll(values, ENC_HD // 2, 1),
+            )
+            return (values * cosine + swapped * sine).astype(BF16)
+
+        for part in range(4):
+            columns = slice(part * 256, (part + 1) * 256)
+            query = jnp.dot(normed, wq_ref[:, columns], preferred_element_type=F32)
+            key = jnp.dot(normed, wk_ref[:, columns], preferred_element_type=F32)
+            value = jnp.dot(normed, wv_ref[:, columns], preferred_element_type=F32).astype(BF16)
+            for pair in range(2):
+                cut = slice(pair * LANES, (pair + 1) * LANES)
+                query_pair = rotate(query[:, cut]) * jnp.asarray(0.125, BF16)
+                key_pair = rotate(key[:, cut])
+                value_pair = value[:, cut]
+                mixed = []
+                for head in range(2):
+                    own = first if head == 0 else jnp.logical_not(first)
+                    scores = lax.dot_general(
+                        jnp.where(own, query_pair, jnp.zeros_like(query_pair)), key_pair,
+                        (((1,), (1,)), ((), ())), preferred_element_type=F32,
+                    )
+                    weights = jnp.exp(scores - jnp.max(scores, axis=-1, keepdims=True))
+                    weights = weights / jnp.sum(weights, axis=-1, keepdims=True)
+                    mixed.append(jnp.dot(weights.astype(BF16), value_pair, preferred_element_type=F32))
+                start = part * 256 + pair * LANES
+                mixed_ref[:, start : start + LANES] = jnp.where(first, mixed[0], mixed[1]).astype(BF16)
+        residual = block.astype(F32) + jnp.dot(mixed_ref[...], wo_ref[...], preferred_element_type=F32)
+        out_ref[...] = root_scale(residual, fgain_ref[...]).astype(BF16)
+
+
+def encode(alive, block, other, weights):
+    return pl.pallas_call(
+        encoder_kernel,
+        out_shape=jax.ShapeDtypeStruct((BLOCK, D_ENC), BF16),
+        in_specs=[SMEM] + [VMEM] * 10,
+        out_specs=VMEM,
+        scratch_shapes=[pltpu.VMEM((BLOCK, D_ENC), BF16)],
+        compiler_params=pltpu.CompilerParams(vmem_limit_bytes=32 * 2**20),
+        cost_estimate=pl.CostEstimate(flops=4 * 10**9, bytes_accessed=9 * 2**20, transcendentals=2**20),
+    )(alive, block, other, *weights)
+
+
+def three_parts(values):
+    high = values.astype(BF16).astype(F32)
+    middle = (values - high).astype(BF16).astype(F32)
+    return high, middle, values - high - middle
+
+
+def cross_kernel(place_ref, own0, own1, own2, other0, other1, other2, *refs):
+    loads, out_ref, query_ref, key_ref, value_ref, total_ref, top_ref, sum_ref = (
+        refs[:8], refs[8], refs[9], refs[10], refs[11], refs[12], refs[13], refs[14])
+    lines = query_ref.shape[1]
+    chip_lines = lines // 8
+    for step in range(4):
+        for side in range(2):
+            load = loads[2 * step + side]
+            chip = place_ref[2 + 2 * step + side]
+            for head in range(HALF_HEADS):
+                start = pl.multiple_of(chip * chip_lines, chip_lines)
+                query_ref[head, pl.ds(start, chip_lines), :] = load[
+                    D_ENC + head * chip_lines : D_ENC + (head + 1) * chip_lines, :]
+    total_ref[...] = jnp.zeros_like(total_ref)
+    sum_ref[...] = jnp.zeros_like(sum_ref)
+    top_ref[...] = jnp.full_like(top_ref, -jnp.inf)
+
+    def add_block(tokens_ref):
+        tokens = tokens_ref[...]
+        for step in range(4):
+            pair = jnp.concatenate([loads[2 * step][:D_ENC, :], loads[2 * step + 1][:D_ENC, :]], axis=1)
+            both = jnp.dot(tokens, pair, preferred_element_type=F32).astype(BF16)
+            for side in range(2):
+                chip = place_ref[2 + 2 * step + side]
+                key_ref[chip] = both[:, side * LANES : (side + 1) * LANES]
+        for head in range(HALF_HEADS):
+            scores = lax.dot_general(
+                query_ref[head], key_ref[head], (((1,), (1,)), ((), ())), preferred_element_type=F32
+            ) * (1.0 / math.sqrt(HEAD_DIM))
+            old_top = top_ref[head]
+            new_top = jnp.maximum(old_top, jnp.max(scores, axis=-1, keepdims=True))
+            weights = jnp.exp(scores - new_top[:, :1])
+            shrink = jnp.exp(old_top - new_top)
+            top_ref[head] = new_top
+            sum_ref[head] = sum_ref[head] * shrink + jnp.sum(weights, axis=-1, keepdims=True)
+            total_ref[head] = total_ref[head] * shrink + jnp.dot(
+                weights.astype(BF16), key_ref[HALF_HEADS + head], preferred_element_type=F32)
+
+    for count_at, group in ((0, (own0, own1, own2)), (1, (other0, other1, other2))):
+        for slot in range(CAP):
+            pl.when(place_ref[count_at] > slot)(functools.partial(add_block, group[slot]))
+
+    lane = lax.broadcasted_iota(jnp.int32, (lines, LANES), 1)
+    notes = jnp.zeros((lines, LANES), F32)
+    for head in range(HALF_HEADS):
+        pieces = three_parts(top_ref[head]) + three_parts(sum_ref[head])
+        for at, piece in enumerate(pieces):
+            notes = jnp.where(lane == 6 * head + at, piece, notes)
+        own_lines = lines // out_ref.shape[0]
+        out_ref[:, head] = total_ref[head].astype(BF16).reshape(out_ref.shape[0], own_lines, LANES)
+    out_ref[:, HALF_HEADS] = notes.astype(BF16).reshape(out_ref.shape[0], own_lines, LANES)
+
+
+def cross(places, place, tokens, loads):
+    lines = places * 16
+    return pl.pallas_call(
+        cross_kernel,
+        out_shape=jax.ShapeDtypeStruct((places, HALF_HEADS + 1, 16, LANES), BF16),
+        in_specs=[SMEM] + [VMEM] * 14,
+        out_specs=VMEM,
+        scratch_shapes=[
+            pltpu.VMEM((HALF_HEADS, lines, LANES), BF16),
+            pltpu.VMEM((KV_HEADS, BLOCK, LANES), BF16),
+            pltpu.VMEM((8, LANES), BF16),
+            pltpu.VMEM((HALF_HEADS, lines, LANES), F32),
+            pltpu.VMEM((HALF_HEADS, lines, LANES), F32),
+            pltpu.VMEM((HALF_HEADS, lines, LANES), F32),
+        ],
+        compiler_params=pltpu.CompilerParams(vmem_limit_bytes=40 * 2**20),
+        cost_estimate=pl.CostEstimate(flops=6 * 10**9, bytes_accessed=8 * 2**20, transcendentals=2**20),
+    )(place, *tokens, *loads)
+
+
+def combine_kernel(parts_ref, out_ref):
+    places = parts_ref.shape[0]
+    for core in range(2):
+        notes = [parts_ref[2 * chip + core, HALF_HEADS].astype(F32) for chip in range(places // 2)]
+        for head in range(HALF_HEADS):
+            at = 6 * head
+            tops = [n[:, at : at + 1] + n[:, at + 1 : at + 2] + n[:, at + 2 : at + 3] for n in notes]
+            sums = [n[:, at + 3 : at + 4] + n[:, at + 4 : at + 5] + n[:, at + 5 : at + 6] for n in notes]
+            top = functools.reduce(jnp.maximum, tops)
+            numerator, denominator = 0.0, 0.0
+            for chip in range(places // 2):
+                share = jnp.exp(tops[chip] - top)
+                numerator += share * parts_ref[2 * chip + core, head].astype(F32)
+                denominator += share * sums[chip]
+            out_ref[2 * head + core] = (numerator / denominator).astype(BF16)
+
+
+def combine(parts):
+    return pl.pallas_call(
+        combine_kernel,
+        out_shape=jax.ShapeDtypeStruct((KV_HEADS, 16, LANES), BF16),
+        in_specs=[VMEM],
+        out_specs=VMEM,
+    )(parts)
+
+
+NEXT_Z = (1, 3, 0, 2)
+
+
+def swap_core(values):
+    return lax.ppermute(values, "ctx", [(i, i ^ 1) for i in range(lax.axis_size("ctx"))])
+
+
+def swap_y(values):
+    return lax.ppermute(values, "ctx", [(i, i ^ 2) for i in range(16)])
+
+
+def round_z(values):
+    return lax.ppermute(values, "ctx", [(i, 4 * NEXT_Z[i // 4] + i % 4) for i in range(16)])
+
+
+def local(context, counts, queries, norm_gain, w_query, w_key, w_value, w_out, final_gain, w_kv):
+    places = lax.axis_size("ctx")
+    me = lax.axis_index("ctx")
+    core = me % 2
+    own_count = lax.dynamic_index_in_dim(counts, me, keepdims=False)
+    other_count = lax.dynamic_index_in_dim(counts, me + 1 - 2 * core, keepdims=False)
+    gives = (own_count == 3) & (other_count == 1)
+    takes = (own_count == 1) & (other_count == 3)
+    own_live = own_count - gives.astype(jnp.int32) + takes.astype(jnp.int32)
+    other_live = other_count + gives.astype(jnp.int32) - takes.astype(jnp.int32)
+    taken = swap_core(context[2])
+
+    split = queries.reshape(4, HALF_HEADS, 2, GROUP, HEAD_DIM).transpose(2, 1, 0, 3, 4)
+    split = split.reshape(2, HALF_HEADS, 16, HEAD_DIM)
+    keep = jnp.where(core == 0, split[0], split[1])
+    give = jnp.where(core == 0, split[1], split[0])
+    got = swap_core(give)
+    chip_rows = jnp.concatenate(
+        [jnp.where(core == 0, keep, got)[:, None], jnp.where(core == 0, got, keep)[:, None]], axis=1
+    ).reshape(HALF_HEADS * 32, HEAD_DIM)
+    load0 = jnp.concatenate([w_kv, chip_rows], axis=0)
+
+    cosine, sine = rotary_lanes()
+    weights = (w_query, w_key, w_value, w_out, norm_gain[None], final_gain[None], cosine, sine)
+    flag = lambda alive, alt: jnp.stack([alive.astype(jnp.int32), alt.astype(jnp.int32)])
+
+    beside0 = swap_y(load0)
+    load1 = round_z(load0)
+    token0 = encode(flag(own_live > 0, own_live < 0), context[0], taken, weights)
+    far0 = swap_core(token0)
+    beside1 = swap_y(load1)
+    load2 = round_z(load1)
+    token1 = encode(flag(own_live > 1, takes), context[1], taken, weights)
+    far1 = swap_core(token1)
+    beside2 = swap_y(load2)
+    load3 = round_z(load2)
+    token2 = encode(flag(own_live > 2, own_live < 0), context[2], taken, weights)
+    far2 = swap_core(token2)
+    beside3 = swap_y(load3)
+
+    z, y = me // 4, me // 2 % 2
+    before = jnp.array([2, 0, 3, 1], jnp.int32)
+    chips = []
+    for _ in range(4):
+        chips += [2 * z + y, 2 * z + 1 - y]
+        z = before[z]
+    place = jnp.stack([own_live, other_live] + chips).astype(jnp.int32)
+    parts = cross(
+        places, place, (token0, token1, token2, far0, far1, far2),
+        (load0, beside0, load1, beside1, load2, beside2, load3, beside3),
+    )
+    parts = lax.all_to_all(parts, "ctx", 0, 0, tiled=True)
+    result = combine(parts)
+    return result.reshape(KV_HEADS, 4, GROUP, HEAD_DIM).transpose(1, 0, 2, 3).reshape(4, QW)
 
 
 def rotary_tables(length, head_width):
@@ -61,7 +314,7 @@
     return (numerator.reshape(total_rows, QW), denominator)
 
 
-def local(context, counts, queries, norm_gain, w_query, w_key, w_value, w_out, final_gain, w_kv):
+def local_any(context, counts, queries, norm_gain, w_query, w_key, w_value, w_out, final_gain, w_kv):
     places = lax.axis_size("ctx")
     device_index = lax.axis_index("ctx")
     device_number = jnp.arange(places)
@@ -132,4 +385,5 @@
         P(None, "ctx"),
     )
     out_specs = P(("groups", "ctx"), None)
-    return jax.shard_map(local, mesh=mesh, in_specs=in_specs, out_specs=out_specs, check_vma=False)
+    small = mesh.shape["ctx"] == 16
+    return jax.shard_map(local if small else local_any, mesh=mesh, in_specs=in_specs, out_specs=out_specs, check_vma=False)

time: 250 us -> 99.5 us (0.40)
  blocking collectives: 113 us -> 15.1 us
  matrix products: 42 us -> 0 us
  Pallas kernels: 0 us -> 28.3 us
  other arithmetic: 26.8 us -> 1.1 us
  waiting for transfers between devices: 29.6 us -> 13.1 us
  starting transfers between devices: 0.04 us -> 11.7 us
  between operations: 14.2 us -> 9.58 us
  local copies, waits for them, and re-layouts: 24 us -> 19.9 us
    unnamed x1 -> x0, blocking collectives: 58 us -> none
    dot_general x8 -> x0, matrix products: 42 us -> none  [the longest x1 10 us: local(): jnp.einsum('shqk,skhd->sqhd', weights, value_rows, preferred_element_type...]
    pmax x1 -> x0, blocking collectives: 30.4 us -> none  [local(): lax.pmax(local_top.astype(jnp.bfloat16), 'ctx').astype(local_top.dtype)]
    unnamed x3 -> x0, waiting for transfers between devices: 29.6 us -> none
    pallas_call x0 -> x5, Pallas kernels: none -> 28.3 us  [the longest x3 16.2 us: encode(): pl.pallas_call(encoder_kernel, out_shape=jax.ShapeDtypeStruct((BLOCK, D_E...]
    all_gather x1 -> x0, blocking collectives: 24.6 us -> none  [local(): every_query = lax.all_gather(queries, 'ctx', axis=0, tiled=True)]
    sub x1 -> x0, other arithmetic: 16.4 us -> none  [local(): weights = jax.nn.softmax(scores, axis=-1).astype(jnp.bfloat16)]
    all_to_all x0 -> x1, blocking collectives: none -> 15.1 us  [local(): parts = lax.all_to_all(parts, 'ctx', 0, 0, tiled=True)]
  transfers between devices with their start and end apart: 2 -> 12, of which waited for: 1 -> 3; matrix products, arithmetic and copies ran while one was open for 28% -> 5% of each run, Pallas kernels for 0% -> 16%
where the time goes in v1:
time: 99.5 us; the launch traced here: 98.8 us
  Pallas kernels  28.3 us (28%)
  local copies, waits for them, and re-layouts  19.9 us (20%)
  blocking collectives  15.1 us (15%)
  waiting for transfers between devices  13.1 us (13%)
  starting transfers between devices  11.7 us (12%)
  between operations  9.58 us (10%)
  other arithmetic  1.1 us (1%)
    pallas_call x3, Pallas kernels, encode(): pl.pallas_call(encoder_kernel, out_shape=jax.ShapeDtypeStruct((BLOCK, D_E...  16.2 us
    all_to_all x1, blocking collectives, local(): parts = lax.all_to_all(parts, 'ctx', 0, 0, tiled=True)  15.1 us
    unnamed x46, local copies, waits for them, and re-layouts  13.6 us
    pallas_call x1, Pallas kernels, cross(): pl.pallas_call(cross_kernel, out_shape=jax.ShapeDtypeStruct((places, HALF...  10 us
    ppermute x3, waiting for transfers between devices, round_z(): lax.ppermute(values, 'ctx', [(i, 4 * NEXT_Z[i // 4] + i % 4) for i in ran...  9.38 us
    ppermute x3, starting transfers between devices, round_z(): lax.ppermute(values, 'ctx', [(i, 4 * NEXT_Z[i // 4] + i % 4) for i in ran...  7.76 us
    ppermute x4, waiting for transfers between devices, swap_y(): return lax.ppermute(values, 'ctx', [(i, i ^ 2) for i in range(16)])  3.71 us
    ppermute x4, starting transfers between devices, swap_y(): return lax.ppermute(values, 'ctx', [(i, i ^ 2) for i in range(16)])  3.11 us
  transfers between devices with their start and end apart: 12, of which 3 were waited for; matrix products, arithmetic and copies ran while one was open for 5% of the time, Pallas kernels for 16%

profile of v1, /device:TPU:0, one launch (start us, length us, event | category | flops | bytes accessed | tf_op | source)
XLA Modules:
  0.0 98.8 jit_solution(8363698548580835403)
XLA Ops:
  0.0 0.8 reshape.33
  1.4 1.5 %slice_bitcast_fusion = (bf16[256,1024]{1,0:T(8,128)(2,1)S(1)}, bf16[256,1024]{1,0:T(8,128)(2,1)S(1)}, bf16[256,1024]{1,0:T(8,128)(2,1)S(1)}) fusion(bf16[3,256,1024]{2,1,0:T(8,128)(2,1)} %param.11), kind=kLoop, calls=%fused_computation | loop fusion | bytes 3145728 | tf_op jit(solution)/shard_map/squeeze | solution.py:258
  7.2 3.1 %collective-permute-start.6 = (bf16[1152,128]{1,0:T(8,128)(2,1)S(1)}, bf16[1152,128]{1,0:T(8,128)(2,1)S(1)}, u32[]{:S(2)}, u32[]{:S(2)}) collective-permute-start(bf16[1152,128]{1,0:T(8,128)(2,1)S(1)} %pad_maximum_fusion.refs_0_), channel_id=1, source_target_pairs={{0,4},{1,5},{2,6},{3,7},{4,12},{5,13},{6,14},{7,15},{8,0},{9,1},{1... | collective-permute-start | bytes 884744 | tf_op jit(solution)/shard_map/ppermute | solution.py:223
  11.1 1.6 %collective-permute-start.5 = (bf16[1152,128]{1,0:T(8,128)(2,1)S(1)}, bf16[1152,128]{1,0:T(8,128)(2,1)S(1)}, u32[]{:S(2)}, u32[]{:S(2)}) collective-permute-start(bf16[1152,128]{1,0:T(8,128)(2,1)S(1)} %pad_maximum_fusion.refs_0_), channel_id=1, source_target_pairs={{0,2},{1,3},{2,0},{3,1},{4,6},{5,7},{6,4},{7,5},{8,10},{9,11},{10,... | collective-permute-start | bytes 884744 | tf_op jit(solution)/shard_map/ppermute | solution.py:219
  12.7 5.8 %collective-permute-done.6.refs_2_ = bf16[1152,128]{1,0:T(8,128)(2,1)S(1)} collective-permute-done((bf16[1152,128]{1,0:T(8,128)(2,1)S(1)}, bf16[1152,128]{1,0:T(8,128)(2,1)S(1)}, u32[]{:S(2)}, u32[]{:S(2)}) %collective-permute-start.6) | collective-permute-done | bytes 294944 | tf_op jit(solution)/shard_map/ppermute | solution.py:223
  18.6 0.8 collective-permute-start.8
  19.4 1.5 %collective-permute-start.7 = (bf16[1152,128]{1,0:T(8,128)(2,1)S(1)}, bf16[1152,128]{1,0:T(8,128)(2,1)S(1)}, u32[]{:S(2)}, u32[]{:S(2)}) collective-permute-start(bf16[1152,128]{1,0:T(8,128)(2,1)S(1)} %collective-permute-done.6.refs_2_), channel_id=1, source_target_pairs={{0,2},{1,3},{2,0},{3,1},{4,6},{5,7},{6,4},{7,5},{8,10},{9,11},{10,... | collective-permute-start | bytes 884744 | tf_op jit(solution)/shard_map/ppermute | solution.py:219
  20.9 1.8 %copy-done = bf16[1024,1024]{1,0:T(8,128)(2,1)S(1)} copy-done((bf16[1024,1024]{1,0:T(8,128)(2,1)S(1)}, bf16[1024,1024]{1,0:T(8,128)(2,1)}, u32[]{:S(2)}) %copy-start) | copy-done | bytes 2097176
  22.7 1.6 %copy-done.2 = bf16[1024,1024]{1,0:T(8,128)(2,1)S(1)} copy-done((bf16[1024,1024]{1,0:T(8,128)(2,1)S(1)}, bf16[1024,1024]{1,0:T(8,128)(2,1)}, u32[]{:S(2)}) %copy-start.2) | copy-done | bytes 2097176
  24.3 1.6 %copy-done.4 = bf16[1024,1024]{1,0:T(8,128)(2,1)S(1)} copy-done((bf16[1024,1024]{1,0:T(8,128)(2,1)S(1)}, bf16[1024,1024]{1,0:T(8,128)(2,1)}, u32[]{:S(2)}) %copy-start.4) | copy-done | bytes 2097176
  25.9 1.6 %copy-done.6 = bf16[1024,1024]{1,0:T(8,128)(2,1)S(1)} copy-done((bf16[1024,1024]{1,0:T(8,128)(2,1)S(1)}, bf16[1024,1024]{1,0:T(8,128)(2,1)}, u32[]{:S(2)}) %copy-start.6) | copy-done | bytes 2097176
  27.5 7.6 %shard_map.109.own0 = bf16[256,1024]{1,0:T(8,128)(2,1)S(1)} custom-call(s32[2]{0:T(128)S(1)} %pad_add_fusion.alive_ref, bf16[256,1024]{1,0:T(8,128)(2,1)S(1)} %get-tuple-element.6.x_ref, bf16[256,1024]{1,0:T(8,128)(2,1)S(1)} %collective-permute-done.alt_ref, bf16[1024,1024]{1,0:T(8,128)(2,1)S(1)} %copy-done, bf16[1024,1024]{1,0:T(8,128)(2,1)S(1)} %copy-done.2, ...), custom_call_target="tpu_custom_call" | custom-call | flops 4000000000 | bytes 9437184 | tf_op jit(solution)/shard_map/pallas_call | solution.py:95
  35.3 7.8 %shard_map.110.own1 = bf16[256,1024]{1,0:T(8,128)(2,1)S(1)} custom-call(s32[2]{0:T(128)S(1)} %pad_add_fusion.1.alive_ref, bf16[256,1024]{1,0:T(8,128)(2,1)S(1)} %get-tuple-element.5.x_ref, bf16[256,1024]{1,0:T(8,128)(2,1)S(1)} %collective-permute-done.alt_ref, bf16[1024,1024]{1,0:T(8,128)(2,1)S(1)} %copy-done.1, bf16[1024,1024]{1,0:T(8,128)(2,1)S(1)} %copy-done.3, ...), custom_call_target="tpu_custom_call" | custom-call | flops 4000000000 | bytes 9437184 | tf_op jit(solution)/shard_map/pallas_call | solution.py:95
  43.2 3.8 %collective-permute-start.10 = (bf16[1152,128]{1,0:T(8,128)(2,1)}, bf16[1152,128]{1,0:T(8,128)(2,1)}, u32[]{:S(2)}, u32[]{:S(2)}) collective-permute-start(bf16[1152,128]{1,0:T(8,128)(2,1)} %collective-permute-done.8.refs_4_), channel_id=1, source_target_pairs={{0,4},{1,5},{2,6},{3,7},{4,12},{5,13},{6,14},{7,15},{8,0},{9,1},{1... | collective-permute-start | bytes 884744 | tf_op jit(solution)/shard_map/ppermute | solution.py:223
  47.0 1.0 %copy-done.9 = bf16[256,1024]{1,0:T(8,128)(2,1)S(1)} copy-done((bf16[256,1024]{1,0:T(8,128)(2,1)S(1)}, bf16[256,1024]{1,0:T(8,128)(2,1)}, u32[]{:S(2)}) %copy-start.9) | copy-done | bytes 524312
  50.3 3.6 %collective-permute-done.10.refs_6_ = bf16[1152,128]{1,0:T(8,128)(2,1)} collective-permute-done((bf16[1152,128]{1,0:T(8,128)(2,1)}, bf16[1152,128]{1,0:T(8,128)(2,1)}, u32[]{:S(2)}, u32[]{:S(2)}) %collective-permute-start.10) | collective-permute-done | bytes 294944 | tf_op jit(solution)/shard_map/ppermute | solution.py:223
  62.6 3.7 %collective-permute-done.11.refs_7_ = bf16[1152,128]{1,0:T(8,128)(2,1)} collective-permute-done((bf16[1152,128]{1,0:T(8,128)(2,1)}, bf16[1152,128]{1,0:T(8,128)(2,1)}, u32[]{:S(2)}, u32[]{:S(2)}) %collective-permute-start.11) | collective-permute-done | bytes 294944 | tf_op jit(solution)/shard_map/ppermute | solution.py:219
  66.3 1.0 copy-done.11
  67.3 1.0 copy-done.13
  68.2 1.0 copy-done.15
  69.2 1.0 copy-done.17
  70.2 10.0 %shard_map.112 = bf16[16,5,16,128]{3,2,1,0:T(8,128)(2,1)S(1)} custom-call(s32[10]{0:T(128)S(1)} %stack.80.place_ref, bf16[256,1024]{1,0:T(8,128)(2,1)S(1)} %shard_map.109.own0, bf16[256,1024]{1,0:T(8,128)(2,1)S(1)} %shard_map.110.own1, bf16[256,1024]{1,0:T(8,128)(2,1)S(1)} %shard_map.111.own2, bf16[256,1024]{1,0:T(8,128)(2,1)S(1)} %collective-permute-done.1.other0, ...), custom_call_target="tpu_custom_call" | custom-call | flops 6000000000 | bytes 8388608 | tf_op jit(solution)/shard_map/pallas_call | solution.py:167
  80.2 15.1 %all_to_all.5.parts_ref = bf16[16,5,16,128]{3,2,1,0:T(8,128)(2,1)} all-to-all(bf16[16,5,16,128]{3,2,1,0:T(8,128)(2,1)S(1)} %shard_map.112), channel_id=1, replica_groups=mesh['groups'=2,'ctx'=16] {'ctx'}, dimensions={0} | all-to-all | bytes 655360 | tf_op jit(solution)/shard_map/all_to_all | solution.py:277
  95.3 2.1 %shard_map.113 = bf16[8,16,128]{2,1,0:T(8,128)(2,1)} custom-call(bf16[16,5,16,128]{3,2,1,0:T(8,128)(2,1)} %all_to_all.5.parts_ref), custom_call_target="tpu_custom_call" | custom-call | tf_op jit(solution)/shard_map/pallas_call | solution.py:203
  (76 shorter events, 8.9 us)
Async XLA Ops:
  0.0 3.0 %copy-start.21 = (s32[16]{0:T(128)S(1)}, s32[16]{0:T(128)}, u32[]{:S(2)}) copy-start(s32[16]{0:T(128)} %param.12) | copy-start | bytes 196
  0.0 7.1 %copy-start.19 = (bf16[1024]{0:T(1024)(128)(2,1)S(1)}, bf16[1024]{0:T(1024)(128)(2,1)}, u32[]{:S(2)}) copy-start(bf16[1024]{0:T(1024)(128)(2,1)} %param.14) | copy-start | bytes 6148
  0.0 7.1 %copy-start.20 = (bf16[1024]{0:T(1024)(128)(2,1)S(1)}, bf16[1024]{0:T(1024)(128)(2,1)}, u32[]{:S(2)}) copy-start(bf16[1024]{0:T(1024)(128)(2,1)} %param.19) | copy-start | bytes 6148
  0.0 7.2 %copy-start.18 = (bf16[1024,128]{1,0:T(8,128)(2,1)S(1)}, bf16[1024,128]{1,0:T(8,128)(2,1)}, u32[]{:S(2)}) copy-start(bf16[1024,128]{1,0:T(8,128)(2,1)} %param.20) | copy-start | bytes 786436
  0.9 6.3 %collective-permute-start.4 = (bf16[4,16,128]{2,1,0:T(8,128)(2,1)S(1)}, bf16[4,16,128]{2,1,0:T(8,128)(2,1)S(1)}, u32[]{:S(2)}, u32[]{:S(2)}) collective-permute-start(bf16[4,16,128]{2,1,0:T(8,128)(2,1)S(1)} %bitcast.43), channel_id=1, source_target_pairs={{0,1},{1,0},{2,3},{3,2},{4,5},{5,4},{6,7},{7,6},{8,9},{9,8},{10,11... | collective-permute-start | bytes 49160 | tf_op jit(solution)/shard_map/ppermute | solution.py:215
  2.9 18.0 %collective-permute-start = (bf16[256,1024]{1,0:T(8,128)(2,1)S(1)}, bf16[256,1024]{1,0:T(8,128)(2,1)S(1)}, u32[]{:S(2)}, u32[]{:S(2)}) collective-permute-start(bf16[256,1024]{1,0:T(8,128)(2,1)S(1)} %get-tuple-element.7.x_ref), channel_id=1, source_target_pairs={{0,1},{1,0},{2,3},{3,2},{4,5},{5,4},{6,7},{7,6},{8,9},{9,8},{10,11... | collective-permute-start | bytes 1572872 | tf_op jit(solution)/shard_map/ppermute | solution.py:215
  7.2 11.3 %collective-permute-start.6 = (bf16[1152,128]{1,0:T(8,128)(2,1)S(1)}, bf16[1152,128]{1,0:T(8,128)(2,1)S(1)}, u32[]{:S(2)}, u32[]{:S(2)}) collective-permute-start(bf16[1152,128]{1,0:T(8,128)(2,1)S(1)} %pad_maximum_fusion.refs_0_), channel_id=1, source_target_pairs={{0,4},{1,5},{2,6},{3,7},{4,12},{5,13},{6,14},{7,15},{8,0},{9,1},{1... | collective-permute-start | bytes 884744 | tf_op jit(solution)/shard_map/ppermute | solution.py:223
  11.1 37.7 %collective-permute-start.5 = (bf16[1152,128]{1,0:T(8,128)(2,1)S(1)}, bf16[1152,128]{1,0:T(8,128)(2,1)S(1)}, u32[]{:S(2)}, u32[]{:S(2)}) collective-permute-start(bf16[1152,128]{1,0:T(8,128)(2,1)S(1)} %pad_maximum_fusion.refs_0_), channel_id=1, source_target_pairs={{0,2},{1,3},{2,0},{3,1},{4,6},{5,7},{6,4},{7,5},{8,10},{9,11},{10,... | collective-permute-start | bytes 884744 | tf_op jit(solution)/shard_map/ppermute | solution.py:219
  18.6 16.6 %copy-start.10 = (bf16[1152,128]{1,0:T(8,128)(2,1)}, bf16[1152,128]{1,0:T(8,128)(2,1)S(1)}, u32[]{:S(2)}) copy-start(bf16[1152,128]{1,0:T(8,128)(2,1)S(1)} %collective-permute-done.6.refs_2_) | copy-start | bytes 884740
  18.6 24.6 %collective-permute-start.8 = (bf16[1152,128]{1,0:T(8,128)(2,1)S(1)}, bf16[1152,128]{1,0:T(8,128)(2,1)}, u32[]{:S(2)}, u32[]{:S(2)}) collective-permute-start(bf16[1152,128]{1,0:T(8,128)(2,1)S(1)} %collective-permute-done.6.refs_2_), channel_id=1, source_target_pairs={{0,4},{1,5},{2,6},{3,7},{4,12},{5,13},{6,14},{7,15},{8,0},{9,1},{1... | collective-permute-start | bytes 884744 | tf_op jit(solution)/shard_map/ppermute | solution.py:223
  19.4 30.1 %collective-permute-start.7 = (bf16[1152,128]{1,0:T(8,128)(2,1)S(1)}, bf16[1152,128]{1,0:T(8,128)(2,1)S(1)}, u32[]{:S(2)}, u32[]{:S(2)}) collective-permute-start(bf16[1152,128]{1,0:T(8,128)(2,1)S(1)} %collective-permute-done.6.refs_2_), channel_id=1, source_target_pairs={{0,2},{1,3},{2,0},{3,1},{4,6},{5,7},{6,4},{7,5},{8,10},{9,11},{10,... | collective-permute-start | bytes 884744 | tf_op jit(solution)/shard_map/ppermute | solution.py:219
  20.9 14.3 %copy-start.8 = (bf16[256,1024]{1,0:T(8,128)(2,1)}, bf16[256,1024]{1,0:T(8,128)(2,1)S(1)}, u32[]{:S(2)}) copy-start(bf16[256,1024]{1,0:T(8,128)(2,1)S(1)} %collective-permute-done.alt_ref) | copy-start | bytes 1572868
  20.9 1.8 %copy-start = (bf16[1024,1024]{1,0:T(8,128)(2,1)S(1)}, bf16[1024,1024]{1,0:T(8,128)(2,1)}, u32[]{:S(2)}) copy-start(bf16[1024,1024]{1,0:T(8,128)(2,1)} %wq_ref.5) | copy-start | bytes 6291460
  27.5 7.7 %copy-start.1 = (bf16[1024,1024]{1,0:T(8,128)(2,1)S(1)}, bf16[1024,1024]{1,0:T(8,128)(2,1)}, u32[]{:S(2)}) copy-start(bf16[1024,1024]{1,0:T(8,128)(2,1)} %wq_ref.5) | copy-start | bytes 6291460
  27.5 7.7 %copy-start.3 = (bf16[1024,1024]{1,0:T(8,128)(2,1)S(1)}, bf16[1024,1024]{1,0:T(8,128)(2,1)}, u32[]{:S(2)}) copy-start(bf16[1024,1024]{1,0:T(8,128)(2,1)} %wk_ref.5) | copy-start | bytes 6291460
  27.5 7.8 %copy-start.5 = (bf16[1024,1024]{1,0:T(8,128)(2,1)S(1)}, bf16[1024,1024]{1,0:T(8,128)(2,1)}, u32[]{:S(2)}) copy-start(bf16[1024,1024]{1,0:T(8,128)(2,1)} %wv_ref.5) | copy-start | bytes 6291460
  27.5 7.8 %copy-start.7 = (bf16[1024,1024]{1,0:T(8,128)(2,1)S(1)}, bf16[1024,1024]{1,0:T(8,128)(2,1)}, u32[]{:S(2)}) copy-start(bf16[1024,1024]{1,0:T(8,128)(2,1)} %wo_ref.5) | copy-start | bytes 6291460
  35.1 27.5 %collective-permute-start.1 = (bf16[256,1024]{1,0:T(8,128)(2,1)S(1)}, bf16[256,1024]{1,0:T(8,128)(2,1)S(1)}, u32[]{:S(2)}, u32[]{:S(2)}) collective-permute-start(bf16[256,1024]{1,0:T(8,128)(2,1)S(1)} %shard_map.109.own0), channel_id=1, source_target_pairs={{0,1},{1,0},{2,3},{3,2},{4,5},{5,4},{6,7},{7,6},{8,9},{9,8},{10,11... | collective-permute-start | bytes 1572872 | tf_op jit(solution)/shard_map/ppermute | solution.py:215
  35.3 18.6 %copy-start.22 = (s32[4]{0:T(128)S(1)}, s32[4]{0:T(128)}, u32[]{:S(2)}) copy-start(s32[4]{0:T(128)} %constant.59.clone) | copy-start | bytes 52
  43.1 19.5 %collective-permute-start.2 = (bf16[256,1024]{1,0:T(8,128)(2,1)S(1)}, bf16[256,1024]{1,0:T(8,128)(2,1)S(1)}, u32[]{:S(2)}, u32[]{:S(2)}) collective-permute-start(bf16[256,1024]{1,0:T(8,128)(2,1)S(1)} %shard_map.110.own1), channel_id=1, source_target_pairs={{0,1},{1,0},{2,3},{3,2},{4,5},{5,4},{6,7},{7,6},{8,9},{9,8},{10,11... | collective-permute-start | bytes 1572872 | tf_op jit(solution)/shard_map/ppermute | solution.py:215
  43.2 10.6 %collective-permute-start.10 = (bf16[1152,128]{1,0:T(8,128)(2,1)}, bf16[1152,128]{1,0:T(8,128)(2,1)}, u32[]{:S(2)}, u32[]{:S(2)}) collective-permute-start(bf16[1152,128]{1,0:T(8,128)(2,1)} %collective-permute-done.8.refs_4_), channel_id=1, source_target_pairs={{0,4},{1,5},{2,6},{3,7},{4,12},{5,13},{6,14},{7,15},{8,0},{9,1},{1... | collective-permute-start | bytes 884744 | tf_op jit(solution)/shard_map/ppermute | solution.py:223
  49.5 13.1 %collective-permute-start.3 = (bf16[256,1024]{1,0:T(8,128)(2,1)S(1)}, bf16[256,1024]{1,0:T(8,128)(2,1)}, u32[]{:S(2)}, u32[]{:S(2)}) collective-permute-start(bf16[256,1024]{1,0:T(8,128)(2,1)S(1)} %shard_map.111.own2), channel_id=1, source_target_pairs={{0,1},{1,0},{2,3},{3,2},{4,5},{5,4},{6,7},{7,6},{8,9},{9,8},{10,11... | collective-permute-start | bytes 1572872 | tf_op jit(solution)/shard_map/ppermute | solution.py:215
  50.2 11.6 %collective-permute-start.9 = (bf16[1152,128]{1,0:T(8,128)(2,1)}, bf16[1152,128]{1,0:T(8,128)(2,1)S(1)}, u32[]{:S(2)}, u32[]{:S(2)}) collective-permute-start(bf16[1152,128]{1,0:T(8,128)(2,1)} %collective-permute-done.8.refs_4_), channel_id=1, source_target_pairs={{0,2},{1,3},{2,0},{3,1},{4,6},{5,7},{6,4},{7,5},{8,10},{9,11},{10,... | collective-permute-start | bytes 884744 | tf_op jit(solution)/shard_map/ppermute | solution.py:219
  53.8 12.5 %collective-permute-start.11 = (bf16[1152,128]{1,0:T(8,128)(2,1)}, bf16[1152,128]{1,0:T(8,128)(2,1)}, u32[]{:S(2)}, u32[]{:S(2)}) collective-permute-start(bf16[1152,128]{1,0:T(8,128)(2,1)} %collective-permute-done.10.refs_6_), channel_id=1, source_target_pairs={{0,2},{1,3},{2,0},{3,1},{4,6},{5,7},{6,4},{7,5},{8,10},{9,11},{10,... | collective-permute-start | bytes 884744 | tf_op jit(solution)/shard_map/ppermute | solution.py:219
  (11 other events, 11.8 us)
